TPU v7x, 256 devices: a whole 4x4x8 slice. The times are simulated.
256 devices in a mesh: row: 4 (over x), ta: 64 (over z, y, core).
Axes of the slice: x: 4, y: 4, z: 8, core: 2. Of those that a mesh axis runs over, the one named last changes fastest.
Arguments:
- grid: bfloat16 [64, 512, 2048], P('row', 'ta'), may hold values from -6 to 6
- omega: float32 [64, 512], P('row', 'ta'), may hold values from -0.002 to 0.002
- legendre_weights: bfloat16 [512, 512, 256], P('ta', 'row'), may hold values from -1 to 1, as said below
- radial_inverses: float32 [512, 4096], P('row'), may hold values from -1 to 2
Outputs:
- new_spectrum: bfloat16 [512, 512, 256], P('ta', 'row')
Inputs may be any that keep to these rules, and one draw needn't show every extreme that they name: legendre_weights[s, k, :] is zero wherever l(k) < m(s).
All inputs are finite; a program needn't handle non-finite values.
Results may differ from a plain program's by a relative error of at most 0.0059.
Values may be sent and summed in bfloat16 or wider, within the bound.
A program may use at most 64 MiB of HBM per device.

v0:
```python
import jax
import jax.numpy as jnp
from jax import lax
from jax.sharding import PartitionSpec as P

M = 512
NR = 64


def project(weights, even_input, odd_input):
    slot_count, degree_span, lat_count = weights.shape
    paired = weights.reshape(slot_count, degree_span // 2, 2, lat_count)
    even_part = jnp.einsum(
        "slt,stc->slc", paired[:, :, 0], even_input, preferred_element_type=jnp.float32
    )
    odd_part = jnp.einsum(
        "slt,stc->slc", paired[:, :, 1], odd_input, preferred_element_type=jnp.float32
    )
    return jnp.stack([even_part, odd_part], 2).reshape(slot_count, degree_span, even_input.shape[2])


def shards(grid, omega, legendre_weights, radial_inverses):
    task_count = lax.axis_size("ta")
    local_radii, local_lats, columns = grid.shape
    positions = jnp.arange(M)
    pair_index = positions // 2
    orders = jnp.where(positions % 2 == 0, pair_index, M - 1 - pair_index).astype(jnp.float32)
    values = grid.reshape(local_radii, local_lats, M, 2, 2).astype(jnp.float32)
    rotation = (omega[:, :, None] * orders[None, None, :])[..., None]
    real_part = values[..., 0]
    imag_part = values[..., 1]
    forced = jnp.stack([real_part + rotation * imag_part, imag_part - rotation * real_part], -1)
    forced = forced.reshape(local_radii, local_lats, columns).astype(jnp.bfloat16)
    slot_block = M // task_count
    degree_count = legendre_weights.shape[1]
    half_lats = legendre_weights.shape[2]
    slot_index = lax.axis_index("ta") * slot_block + jnp.arange(slot_block)
    slot_pairs = slot_index // 2
    local_orders = jnp.where(slot_index % 2 == 0, slot_pairs, M - 1 - slot_pairs)
    even_order = (local_orders % 2 == 0)[:, None, None]
    gathered = lax.all_gather(forced, "row", axis=0, tiled=True)
    moved = lax.all_to_all(gathered, "ta", split_axis=2, concat_axis=1, tiled=True)
    radius_count = moved.shape[0]
    shaped = moved.reshape(radius_count, 2 * half_lats, slot_block, 4)
    northern = shaped[:, :half_lats].astype(jnp.float32)
    southern = shaped[:, half_lats:][:, ::-1].astype(jnp.float32)
    symmetric = jnp.transpose((northern + southern).astype(jnp.bfloat16), (2, 1, 0, 3))
    symmetric = symmetric.reshape(slot_block, half_lats, radius_count * 4)
    antisym = jnp.transpose((northern - southern).astype(jnp.bfloat16), (2, 1, 0, 3))
    antisym = antisym.reshape(slot_block, half_lats, radius_count * 4)
    even_input = jnp.where(even_order, symmetric, antisym)
    odd_input = jnp.where(even_order, antisym, symmetric)
    spectrum = project(legendre_weights, even_input, odd_input)
    spectrum = spectrum.reshape(slot_block, degree_count, NR, 4)
    inverses = radial_inverses.reshape(degree_count, NR, NR)
    solved = jnp.einsum(
        "lab,slbc->slac",
        inverses,
        spectrum,
        precision=lax.Precision.HIGHEST,
        preferred_element_type=jnp.float32,
    )
    return solved.reshape(slot_block, degree_count, NR * 4).astype(jnp.bfloat16)


def solution(mesh):
    in_specs = (P("row", "ta", None), P("row", "ta"), P("ta", "row", None), P("row", None))
    out_specs = P("ta", "row", None)
    return jax.shard_map(shards, mesh=mesh, in_specs=in_specs, out_specs=out_specs, check_vma=False)
```

profile of v0, /device:TPU:1, one launch (start us, length us, event | category | flops | bytes accessed | tf_op | source)
XLA Modules:
  0.0 238.8 jit_solution(16314047392707123849)
XLA Ops:
  6.5 0.0 all-gather.2.cloned.1.call-start
  6.5 0.0 copy-start.3
  6.5 6.0 %copy.42 = f32[16,8,2048]{0,1,2:T(8,128)} copy(bf16[16,8,2048]{2,1,0:T(8,128)(2,1)} %param.4) | data formatting | bytes 1572864 | tf_op jit(solution)/shard_map/convert_element_type | solution.py:28
  12.6 0.0 copy-done.3
  12.6 0.6 broadcast_multiply_fusion
  13.2 6.0 %multiply_add_fusion = (bf16[16,8,512,2,1]{0,1,4,3,2:T(8,128)(2,1)}, bf16[16,8,512,2,1]{0,1,4,3,2:T(8,128)(2,1)S(1)}) fusion(f32[16,8,512,2,2]{0,1,4,3,2:T(8,128)} %bitcast.42, f32[16,8,512]{0,1,2:T(8,128)S(1)} %broadcast_multiply_fusion), kind=kLoop, calls=%fused_computation.7 | loop fusion | flops 786432 | bytes 1835008 | tf_op jit(solution)/shard_map/add | solution.py:32
  19.2 2.8 %copy.43 = bf16[16,8,512,2,1]{2,1,4,3,0:T(8,128)(2,1)S(1)} copy(bf16[16,8,512,2,1]{0,1,4,3,2:T(8,128)(2,1)} %get-tuple-element.5) | data formatting | bytes 524288 | tf_op jit(solution)/shard_map/add | solution.py:32
  22.1 1.9 copy.44
  24.0 6.6 %copy.45 = bf16[16,8,512,2,2]{0,1,4,3,2:T(8,128)(2,1)} copy(bf16[16,8,512,2,2]{2,1,4,3,0:T(8,128)(2,1)S(1)} %pad_maximum_fusion.1) | data formatting | bytes 1048576 | tf_op jit(solution)/shard_map/stack | solution.py:32
  30.6 5.6 %copy.46 = bf16[16,8,2048]{2,1,0:T(8,128)(2,1)} copy(bf16[16,8,2048]{0,1,2:T(8,128)(2,1)} %bitcast.43) | data formatting | bytes 1048576 | tf_op jit(solution)/shard_map/convert_element_type | solution.py:33
  36.2 0.0 all-gather.2.cloned.1.call-update
  36.3 37.3 %all-gather.2.cloned.1.call-done = bf16[64,8,2048]{2,1,0:T(8,128)(2,1)} async-done(((bf16[16,8,2048]{2,1,0:T(8,128)(2,1)}), bf16[64,8,2048]{2,1,0:T(8,128)(2,1)}) %all-gather.2.cloned.1.call-update) | async-done | bytes 2097168 | tf_op jit(solution)/shard_map/all_gather | solution.py:41
  73.6 6.7 %copy.47 = bf16[64,8,2048]{0,1,2:T(8,128)(2,1)} copy(bf16[64,8,2048]{2,1,0:T(8,128)(2,1)} %all-gather.2.cloned.1.call-done) | data formatting | bytes 4194304 | tf_op jit(solution)/shard_map/all_gather | solution.py:41
  80.3 0.0 copy-start.2
  80.3 7.9 %reshape.101 = bf16[64,2,8192]{2,1,0:T(2,128)(2,1)} reshape(bf16[2048,8,64]{2,1,0:T(8,128)(2,1)} %bitcast.44) | data formatting | bytes 4194304
  88.2 10.7 %all-to-all-start = ((bf16[64,2,8192]{2,1,0:T(2,128)(2,1)}), bf16[64,2,8192]{2,1,0:T(2,128)(2,1)S(1)}, u32[]{:S(2)}, u32[]{:S(2)}) async-start(bf16[64,2,8192]{2,1,0:T(2,128)(2,1)} %reshape.101), calls=%async_computation | async-start | bytes 4194304 | tf_op jit(solution)/shard_map/all_to_all | solution.py:42
  98.9 0.0 copy-done.2
  98.9 0.3 copy.52
  99.2 2.9 %copy.58 = f32[128,4096]{0,1:T(8,128)} copy(f32[128,4096]{1,0:T(8,128)} %param.7) | data formatting | bytes 4194304 | tf_op args[3]
  102.2 5.6 %copy.63 = f32[128,64,64,1]{2,1,3,0:T(8,128)} copy(f32[128,64,64,1]{0,2,1,3:T(8,128)} %bitcast.48) | data formatting | bytes 4194304 | tf_op jit(solution)/shard_map/reshape | solution.py:55
  107.7 0.7 fusion.25
  108.5 40.1 %all-to-all-done = bf16[64,2,8192]{2,1,0:T(2,128)(2,1)S(1)} async-done(((bf16[64,2,8192]{2,1,0:T(2,128)(2,1)}), bf16[64,2,8192]{2,1,0:T(2,128)(2,1)S(1)}, u32[]{:S(2)}, u32[]{:S(2)}) %all-to-all-start) | async-done | bytes 2097184 | tf_op jit(solution)/shard_map/all_to_all | solution.py:42
  148.6 4.0 %reshape.102 = bf16[2048,8,64]{2,1,0:T(8,128)(2,1)} reshape(bf16[64,2,8192]{2,1,0:T(2,128)(2,1)S(1)} %all-to-all-done) | data formatting | bytes 4194304
  152.6 3.3 %copy.49 = bf16[64,64,8,32]{0,2,1,3:T(8,128)(2,1)S(1)} copy(bf16[64,64,8,32]{0,2,3,1:T(8,128)(2,1)} %bitcast.45) | data formatting | bytes 4194304 | tf_op jit(solution)/shard_map/all_to_all | solution.py:42
  155.9 0.0 copy-start
  155.9 1.9 copy-done
  157.9 0.1 slice.28
  158.0 20.2 %rev.3 = bf16[64,256,8,4]{0,1,3,2:T(8,128)(2,1)} reverse(bf16[64,256,8,4]{0,1,3,2:T(8,128)(2,1)S(1)} %slice.28), dimensions={1} | reverse | bytes 2097152 | tf_op jit(solution)/shard_map/rev | solution.py:46
  178.2 4.8 %fusion.5 = (bf16[8,256,64,4]{2,1,3,0:T(8,128)(2,1)}, bf16[8,256,64,4]{2,1,3,0:T(8,128)(2,1)S(1)}) fusion(bf16[64,256,8,4]{0,1,3,2:T(8,128)(2,1)} %rev.3, bf16[64,512,8,4]{0,1,3,2:T(8,128)(2,1)} %bitcast.47), kind=kLoop, calls=%fused_computation.9 | loop fusion | flops 3145728 | bytes 4194304 | tf_op jit(solution)/shard_map/transpose | solution.py:47
  183.0 2.7 %copy.50 = bf16[8,256,64,4]{1,0,3,2:T(8,128)(2,1)S(1)} copy(bf16[8,256,64,4]{2,1,3,0:T(8,128)(2,1)} %get-tuple-element.7) | data formatting | bytes 2097152 | tf_op jit(solution)/shard_map/transpose | solution.py:47
  185.8 2.4 %copy.51 = bf16[8,256,64,4]{1,0,3,2:T(8,128)(2,1)} copy(bf16[8,256,64,4]{2,1,3,0:T(8,128)(2,1)S(1)} %get-tuple-element.8) | data formatting | bytes 2097152 | tf_op jit(solution)/shard_map/transpose | solution.py:49
  188.2 0.0 copy-start.1
  188.2 1.5 bitcast_select_fusion.1
  189.7 0.0 copy-done.1
  189.7 0.4 convolution_bitcast_fusion.1
  190.1 0.4 convolution_bitcast_fusion
  190.6 0.1 pad_maximum_fusion
  190.7 8.5 %copy.57 = f32[8,64,2,256]{0,3,2,1:T(8,128)} copy(f32[8,64,2,256]{3,1,0,2:T(8,128)S(1)} %pad_maximum_fusion) | data formatting | bytes 2097152 | tf_op jit(solution)/shard_map/stack | solution.py:19
  199.1 30.1 %fusion.9 = bf16[8,128,64,4]{2,0,3,1:T(8,128)(2,1)S(1)} fusion(f32[128,64,64,1]{2,1,3,0:T(8,128)} %copy.63, f32[8,128,64,4]{0,3,2,1:T(4,128)} %bitcast.41), kind=kOutput, calls=%fused_computation.11 | convolution fusion | flops 201588736 | bytes 3670016 | tf_op jit(solution)/shard_map/lab,slbc->slac/dot_general | solution.py:56
  229.3 1.6 copy.61
  230.8 1.1 copy.62
  (3 shorter events, 0.1 us)
Async XLA Ops:
  6.5 67.1 %all-gather.2.cloned.1.call-start = ((), (), s32[]{:S(2)}) async-start(), calls=%async_computation.1 | async-start | bytes 2621440 | tf_op jit(solution)/shard_map/all_gather | solution.py:41
  6.5 6.0 %copy-start.3 = (f32[16,8]{0,1:T(8,128)S(1)}, f32[16,8]{0,1:T(8,128)}, u32[]{:S(2)}) copy-start(f32[16,8]{0,1:T(8,128)} %param.5) | copy-start | bytes 1540
  80.3 18.6 %copy-start.2 = (bf16[8,128,256]{2,1,0:T(8,128)(2,1)S(1)}, bf16[8,128,256]{2,1,0:T(8,128)(2,1)}, u32[]{:S(2)}) copy-start(bf16[8,128,256]{2,1,0:T(8,128)(2,1)} %param.6) | copy-start | bytes 1572868
  88.2 60.4 %all-to-all-start = ((bf16[64,2,8192]{2,1,0:T(2,128)(2,1)}), bf16[64,2,8192]{2,1,0:T(2,128)(2,1)S(1)}, u32[]{:S(2)}, u32[]{:S(2)}) async-start(bf16[64,2,8192]{2,1,0:T(2,128)(2,1)} %reshape.101), calls=%async_computation | async-start | bytes 4194304 | tf_op jit(solution)/shard_map/all_to_all | solution.py:42
  155.9 2.0 copy-start
  188.2 1.5 copy-start.1
Sparse Core Ops, SparseCore 0:
  36.4 37.1 all-gather.1
where the time goes:
time: 240 us; the launch traced here: 239 us
  local copies, waits for them, and re-layouts  93 us (39%)
  waiting for transfers between devices  77.5 us (32%)
  matrix products  31 us (13%)
  between operations  13.5 us (6%)
  other arithmetic  13.1 us (5%)
  starting transfers between devices  10.7 us (4%)
    all_to_all x1, waiting for transfers between devices, shards(): lax.all_to_all(gathered, 'ta', split_axis=2, concat_axis=1, tiled=True)  40.1 us
    all_gather x1, waiting for transfers between devices, shards(): gathered = lax.all_gather(forced, 'row', axis=0, tiled=True)  37.3 us
    dot_general x1, matrix products, shards(): jnp.einsum('lab,slbc->slac', inverses, spectrum, precision=lax.Precision....  30.1 us
    rev x1, local copies, waits for them, and re-layouts, shards(): southern = shaped[:, half_lats:][:, ::-1].astype(jnp.float32)  20.2 us
    unnamed x12, local copies, waits for them, and re-layouts  17.1 us
    all_to_all x1, starting transfers between devices, shards(): lax.all_to_all(gathered, 'ta', split_axis=2, concat_axis=1, tiled=True)  10.7 us
    another operation x1, local copies, waits for them, and re-layouts, project(): jnp.stack([even_part, odd_part], 2)  8.46 us
    all_gather x1, local copies, waits for them, and re-layouts, shards(): gathered = lax.all_gather(forced, 'row', axis=0, tiled=True)  6.7 us
  transfers between devices with their start and end apart: 2, of which 2 were waited for; matrix products, arithmetic and copies ran while one was open for 4% of the time, Pallas kernels for 0%

commit v1 on v0

v1 whole, which is shorter than its diff:
```python
import functools

import jax
import jax.numpy as jnp
from jax import lax
from jax.experimental import pallas as pl
from jax.experimental.pallas import tpu as pltpu
from jax.sharding import PartitionSpec as P

MESH = pl.DeviceIdType.MESH
F32 = jnp.float32
BF16 = jnp.bfloat16
ROWS = 4
LANES = 128


def dot(a, b):
    return jnp.dot(a, b, preferred_element_type=F32)


def iota(shape, dim):
    return lax.broadcasted_iota(jnp.int32, shape, dim)


def one_hot(target, width):
    return jnp.where(target == iota((target.shape[0], width), 1), 1.0, 0.0).astype(BF16)


def kernel(
    tasks, grid_hbm, omega_ref, weights_hbm, inverses_hbm, out_ref,
    grid_v, omega_v, send, recv, weights, flat_inverses, paired_inverses,
    flip, spread, sym_anti, spec_send, spec_recv, merge, upper, lower, upper_out, lower_out, finish,
    grid_sem, inv_sem, own_sem, send_sem, recv_sem, wsend_sem, wrecv_sem, ysend_sem, yrecv_sem, yown_sem,
):
    row = lax.axis_index("row")
    task = lax.axis_index("ta")
    block = tasks
    half_lats = 4 * tasks
    orders = 8 * tasks
    groups = tasks // 4
    diagonal = (4 * task) // block

    def alive(unit, r):
        if unit == 0:
            return True
        return r >= diagonal if unit == 1 else r <= diagonal

    def when(condition):
        return (lambda f: f()) if condition is True else pl.when(condition)

    barrier = pltpu.get_barrier_semaphore()

    @pl.loop(1, tasks)
    def _(offset):
        pl.semaphore_signal(barrier, 1, device_id={"ta": lax.rem(task + offset, tasks)}, device_id_type=MESH)

    for offset in range(1, ROWS):
        pl.semaphore_signal(barrier, 1, device_id={"row": lax.rem(row + offset, ROWS)}, device_id_type=MESH)

    grid_copy = pltpu.make_async_copy(grid_hbm, grid_v, grid_sem)
    grid_copy.start()

    def unit_source(unit, u):
        slot = 2 * u + (1 if unit == 2 else 0)
        first = 0 if unit == 1 else block
        return weights_hbm.at[slot, pl.ds(first, block), :]

    for unit in range(3):
        for u in range(4):
            pltpu.make_async_copy(unit_source(unit, u), weights.at[unit, row, u], own_sem).start()
    for i in range(32):
        pltpu.make_async_copy(
            inverses_hbm.at[:, pl.ds(i * LANES, LANES)], flat_inverses.at[:, i, :], inv_sem
        ).start()

    for r in range(16):
        omega_v[pl.ds(8 * r, 8), :] = jnp.broadcast_to(omega_ref[:, r : r + 1], (8, LANES))
    grid_copy.wait()

    @pl.loop(0, groups)
    def _(group):
        lanes = pl.ds(pl.multiple_of(group * LANES, LANES), LANES)
        values = grid_v[:, :, lanes].astype(F32).reshape(16 * 8, LANES)
        lane = iota((1, LANES), 1)
        slot = group * 32 + lane // 4
        order = jnp.where(slot % 2 == 0, slot // 2, orders - 1 - slot // 2).astype(F32)
        partner = jnp.where(lane % 2 == 0, pltpu.roll(values, LANES - 1, 1), -pltpu.roll(values, 1, 1))
        forced = values + (omega_v[...] * order) * partner
        t0, t1, t2, t3 = (forced[32 * q : 32 * q + 32] for q in range(4))
        left = lane < 64
        a0 = jnp.where(left, t0, pltpu.roll(t2, 64, 1))
        a2 = jnp.where(left, pltpu.roll(t0, 64, 1), t2)
        a1 = jnp.where(left, t1, pltpu.roll(t3, 64, 1))
        a3 = jnp.where(left, pltpu.roll(t1, 64, 1), t3)
        first = (lane // 32) % 2 == 0
        packed = (
            jnp.where(first, a0, pltpu.roll(a1, 32, 1)),
            jnp.where(first, pltpu.roll(a0, 96, 1), a1),
            jnp.where(first, a2, pltpu.roll(a3, 32, 1)),
            jnp.where(first, pltpu.roll(a2, 96, 1), a3),
        )
        for d in range(4):
            send[group * 4 + d, :, :LANES] = packed[d][:16].astype(BF16)
            send[group * 4 + d, :, LANES:] = packed[d][16:].astype(BF16)

    pl.semaphore_wait(barrier, tasks - 1 + ROWS - 1)

    for offset in range(1, ROWS):
        for unit in range(3):

            @when(alive(unit, row))
            def _():
                for u in range(4):
                    pltpu.make_async_remote_copy(
                        src_ref=unit_source(unit, u),
                        dst_ref=weights.at[unit, row, u],
                        send_sem=wsend_sem.at[unit],
                        recv_sem=wrecv_sem.at[offset, unit],
                        device_id={"row": lax.rem(row + offset, ROWS)},
                        device_id_type=MESH,
                    ).start()

    @pl.loop(1, tasks)
    def _(step):
        to = lax.rem(task + step, tasks)
        pltpu.make_async_remote_copy(
            src_ref=send.at[to],
            dst_ref=recv.at[task],
            send_sem=send_sem,
            recv_sem=recv_sem,
            device_id={"ta": to},
            device_id_type=MESH,
        ).start()

    recv[task] = send[task]

    n = half_lats
    flip[...] = one_hot(n - 1 - iota((n, 1), 0), n)
    index = iota((256, 1), 0)
    s, c = (index // 4) % 8, index % 4
    for h in range(2):
        for high in range(2):
            radius = 4 * ((index // 32) % 4) + 2 * (index // LANES) + h
            spread[h, high] = one_hot(jnp.where(s % 2 == high, (s // 2) * 64 + c * 16 + radius, -1), 256)
    index = iota((512, 1), 0)
    for second in range(2):
        column = ((index // 16) % 4) * 64 + (index // LANES) * 16 + index % 16
        merge[second] = one_hot(jnp.where((index // 64) % 2 == second, column, -1), 256)
    index = iota((256, 1), 0)
    kind = (index // 32) % 4
    finish[...] = one_hot((2 * (index % 32) + kind % 2) * 4 + (index // LANES) * 2 + kind // 2, 256)
    upper[...] = jnp.zeros_like(upper)
    lower[...] = jnp.zeros_like(lower)
    for u in range(4):
        out_ref[2 * u + 1, :block, :] = jnp.zeros((block, 256), BF16)

    pltpu.make_async_copy(flat_inverses, flat_inverses, inv_sem).wait()

    @pl.loop(0, 2 * block)
    def _(k):
        b = flat_inverses[k]
        rolled = pltpu.roll(b, 64, 1)
        left = iota((1, LANES), 1) < 64
        paired_inverses[k] = jnp.concatenate(
            [jnp.where(left, b, 0.0), jnp.where(left, rolled, 0.0), jnp.where(left, 0.0, rolled), jnp.where(left, 0.0, b)], 0
        ).astype(BF16)

    pltpu.make_async_copy(weights.at[:, 0], weights.at[:, 0], own_sem).wait()
    for offset in range(1, ROWS):
        source = lax.rem(row + ROWS - offset, ROWS)
        for unit in range(3):

            @when(alive(unit, source))
            def _():
                pltpu.make_async_copy(
                    weights.at[unit, source], weights.at[unit, source], wrecv_sem.at[offset, unit]
                ).wait()

    pltpu.make_async_copy(recv.at[pl.ds(0, tasks - 1)], recv.at[pl.ds(0, tasks - 1)], recv_sem).wait()

    parts = []
    for h in range(2):
        arrived = recv[...].astype(F32)[:, 8 * h : 8 * h + 8, :].reshape(2 * half_lats, 256)
        northern = arrived[:half_lats]
        southern = dot(flip[...], arrived[half_lats:].astype(BF16))
        parts.append(((northern + southern).astype(BF16), (northern - southern).astype(BF16)))
    for high in range(2):
        for which in range(2):
            columns = dot(parts[0][which], spread[0, high]) + dot(parts[1][which], spread[1, high])
            columns = columns.astype(BF16)
            for pair in range(2):
                sym_anti[high, pair, :, pl.ds(which * LANES, LANES)] = columns[:, pair * LANES : (pair + 1) * LANES]

    even_row = iota((4 * block, 1), 0) % 2 == 0
    left = iota((1, LANES), 1) < 64
    for unit in range(3):
        high = 1 if unit == 2 else 0
        for pair in range(2):
            data = sym_anti[high, pair]
            results = []
            for which in range(2):
                both = dot(weights[unit, :, 2 * pair + which].reshape(4 * block, half_lats), data)
                even_order = (which + high) % 2 == 0
                first, second = both[:, :LANES], both[:, LANES:]
                results.append(jnp.where(even_row, first, second) if even_order else jnp.where(even_row, second, first))
            merged = jnp.where(left, results[0], results[1]).astype(BF16)
            spec_send[unit, :, pair] = merged.reshape(4, block, LANES)
        for offset in range(1, ROWS):
            to = lax.rem(row + offset, ROWS)

            @when(alive(unit, to))
            def _():
                pltpu.make_async_remote_copy(
                    src_ref=spec_send.at[unit, to],
                    dst_ref=spec_recv.at[unit, row],
                    send_sem=ysend_sem.at[unit, offset],
                    recv_sem=yrecv_sem.at[unit, offset],
                    device_id={"row": to},
                    device_id_type=MESH,
                ).start()

    spec_recv[:, row] = spec_send[:, row]

    for unit in range(3):

        @when(alive(unit, row))
        def _():
            for offset in range(1, ROWS):
                source = lax.rem(row + ROWS - offset, ROWS)
                pltpu.make_async_copy(
                    spec_recv.at[unit, source], spec_recv.at[unit, source], yrecv_sem.at[unit, offset]
                ).wait()
            for pair in range(2):
                joined = jnp.concatenate([spec_recv[unit, r, pair] for r in range(ROWS)], 1)
                for second in range(2):
                    spectrum = dot(joined, merge[second])
                    for field in range(2):
                        place = (2 * pair + second) * 2 + field
                        part = spectrum[:, field * LANES : (field + 1) * LANES]
                        if unit == 1:
                            lower[pl.ds(place, block, stride=8), :] = part
                        else:
                            upper[pl.ds(place + (8 if unit == 2 else 0), block, stride=16), :] = part

    def solve(lhs, k):
        return lax.dot_general(
            lhs.astype(BF16), paired_inverses[k], (((1,), (1,)), ((), ())), preferred_element_type=F32
        )

    @pl.loop(0, block)
    def _(k):
        solved = solve(upper[pl.ds(pl.multiple_of(k * 16, 16), 16), :], block + k)
        upper_out[pl.ds(k, 16, stride=block), :] = solved

    @pl.loop(0, block)
    def _(k):
        solved = solve(lower[pl.ds(pl.multiple_of(k * 8, 8), 8), :], k)
        lower_out[pl.ds(k, 8, stride=block), :] = solved

    def ordered(ref, place):
        fields = [ref[pl.ds((place + field) * block, block), :] for field in range(2)]
        return dot(jnp.concatenate(fields, 1).astype(BF16), finish[...]).astype(BF16)

    for u in range(4):
        out_ref[2 * u, block:, :] = ordered(upper_out, 2 * u)
        out_ref[2 * u + 1, block:, :] = ordered(upper_out, 8 + 2 * u)
        out_ref[2 * u, :block, :] = ordered(lower_out, 2 * u)

    pltpu.make_async_copy(send.at[pl.ds(0, tasks - 1)], send.at[pl.ds(0, tasks - 1)], send_sem).wait()
    for unit in range(3):

        @when(alive(unit, row))
        def _():
            three = weights.at[unit, pl.ds(0, 3)]
            pltpu.make_async_copy(three, three, wsend_sem.at[unit]).wait()

        for offset in range(1, ROWS):
            to = lax.rem(row + offset, ROWS)

            @when(alive(unit, to))
            def _():
                sent = spec_send.at[unit, to]
                pltpu.make_async_copy(sent, sent, ysend_sem.at[unit, offset]).wait()


def shards(tasks, grid, omega, legendre_weights, radial_inverses):
    block = tasks
    half_lats = 4 * tasks
    any_space = pl.BlockSpec(memory_space=pl.ANY)
    in_vmem = pl.BlockSpec(memory_space=pltpu.VMEM)
    dma = pltpu.SemaphoreType.DMA
    return pl.pallas_call(
        functools.partial(kernel, tasks),
        out_shape=jax.ShapeDtypeStruct(legendre_weights.shape[:2] + (256,), BF16),
        in_specs=[any_space, in_vmem, any_space, any_space],
        out_specs=in_vmem,
        scratch_shapes=[
            pltpu.VMEM((16, 8, 32 * tasks), BF16),
            pltpu.VMEM((128, LANES), F32),
            pltpu.VMEM((tasks, 16, 256), BF16),
            pltpu.VMEM((tasks, 16, 256), BF16),
            pltpu.VMEM((3, ROWS, 4, block, half_lats), BF16),
            pltpu.VMEM((2 * block, 32, LANES), F32),
            pltpu.VMEM((2 * block, LANES, LANES), BF16),
            pltpu.VMEM((half_lats, half_lats), BF16),
            pltpu.VMEM((2, 2, 256, 256), BF16),
            pltpu.VMEM((2, 2, half_lats, 256), BF16),
            pltpu.VMEM((3, ROWS, 2, block, LANES), BF16),
            pltpu.VMEM((3, ROWS, 2, block, LANES), BF16),
            pltpu.VMEM((2, 512, 256), BF16),
            pltpu.VMEM((block * 16, LANES), F32),
            pltpu.VMEM((block * 8, LANES), F32),
            pltpu.VMEM((block * 16, LANES), F32),
            pltpu.VMEM((block * 8, LANES), F32),
            pltpu.VMEM((256, 256), BF16),
            dma, dma, dma, dma, dma,
            dma((3,)), dma((ROWS, 3)), dma((3, ROWS)), dma((3, ROWS)), dma,
        ],
        compiler_params=pltpu.CompilerParams(
            collective_id=0, has_side_effects=True, vmem_limit_bytes=48 * 1024 * 1024
        ),
    )(grid, omega.T, legendre_weights, radial_inverses)


def solution(mesh):
    in_specs = (P("row", "ta", None), P("row", "ta"), P("ta", "row", None), P("row", None))
    out_specs = P("ta", "row", None)
    return jax.shard_map(
        functools.partial(shards, mesh.shape["ta"]), mesh=mesh, in_specs=in_specs, out_specs=out_specs, check_vma=False
    )
```

time: 240 us -> 63 us (0.26)
  local copies, waits for them, and re-layouts: 93 us -> 5.15 us
  waiting for transfers between devices: 77.5 us -> 0 us
  Pallas kernels: 0 us -> 56.7 us
  matrix products: 31 us -> 0 us
  between operations: 13.5 us -> 0.01 us
  other arithmetic: 13.1 us -> 0 us
  starting transfers between devices: 10.7 us -> 0 us
    pallas_call x0 -> x1, Pallas kernels: none -> 56.7 us  [shards(): pl.pallas_call(functools.partial(kernel, tasks), out_shape=jax.ShapeDtype...]
    all_to_all x1 -> x0, waiting for transfers between devices: 40.1 us -> none  [shards(): lax.all_to_all(gathered, 'ta', split_axis=2, concat_axis=1, tiled=True)]
    all_gather x1 -> x0, waiting for transfers between devices: 37.3 us -> none  [shards(): gathered = lax.all_gather(forced, 'row', axis=0, tiled=True)]
    dot_general x3 -> x0, matrix products: 31 us -> none  [the longest x1 30.1 us: shards(): jnp.einsum('lab,slbc->slac', inverses, spectrum, precision=lax.Precision....]
    rev x1 -> x0, local copies, waits for them, and re-layouts: 20.2 us -> none  [shards(): southern = shaped[:, half_lats:][:, ::-1].astype(jnp.float32)]
    another operation x2 -> x0, local copies, waits for them, and re-layouts: 15 us -> none  [the longest x1 8.46 us: project(): jnp.stack([even_part, odd_part], 2)]
    convert_element_type x4 -> x0, local copies, waits for them, and re-layouts: 14.3 us -> none  [the longest x1 6.03 us: shards(): values = grid.reshape(local_radii, local_lats, M, 2, 2).astype(jnp.float32)]
    unnamed x12 -> x9, local copies, waits for them, and re-layouts: 17.1 us -> 5.15 us
  transfers between devices with their start and end apart: 2 -> 0, of which waited for: 2 -> 0; matrix products, arithmetic and copies ran while one was open for 4% -> 0% of each run, Pallas kernels for 0% -> 0%
where the time goes in v1:
time: 63 us; the launch traced here: 61.9 us
  Pallas kernels  56.7 us (90%)
  local copies, waits for them, and re-layouts  5.15 us (8%)
    pallas_call x1, Pallas kernels, shards(): pl.pallas_call(functools.partial(kernel, tasks), out_shape=jax.ShapeDtype...  56.7 us
    unnamed x9, local copies, waits for them, and re-layouts  5.15 us

profile of v1, /device:TPU:1, one launch (start us, length us, event | category | flops | bytes accessed | tf_op | source)
XLA Modules:
  0.0 61.9 jit_solution(3692369030290777515)
XLA Ops:
  0.0 0.0 copy-start
  0.0 1.6 %copy-done = f32[128,4096]{1,0:T(8,128)S(1)} copy-done((f32[128,4096]{1,0:T(8,128)S(1)}, f32[128,4096]{1,0:T(8,128)}, u32[]{:S(2)}) %copy-start) | copy-done | bytes 2097176
  1.6 0.0 copy-start.1
  1.6 1.0 %copy-done.1 = bf16[16,8,2048]{2,1,0:T(8,128)(2,1)S(1)} copy-done((bf16[16,8,2048]{2,1,0:T(8,128)(2,1)S(1)}, bf16[16,8,2048]{2,1,0:T(8,128)(2,1)}, u32[]{:S(2)}) %copy-start.1) | copy-done | bytes 524312
  2.6 0.0 copy-start.2
  2.6 1.0 %copy-done.2 = bf16[8,128,256]{2,1,0:T(8,128)(2,1)S(1)} copy-done((bf16[8,128,256]{2,1,0:T(8,128)(2,1)S(1)}, bf16[8,128,256]{2,1,0:T(8,128)(2,1)}, u32[]{:S(2)}) %copy-start.2) | copy-done | bytes 524312
  3.7 0.0 copy-start.3
  3.7 0.7 %copy-done.3 = f32[16,8]{0,1:T(8,128)S(1)} copy-done((f32[16,8]{0,1:T(8,128)S(1)}, f32[16,8]{0,1:T(8,128)}, u32[]{:S(2)}) %copy-start.3) | copy-done | bytes 536
  4.4 56.7 %shard_map.46 = bf16[8,128,256]{2,1,0:T(8,128)(2,1)S(1)} custom-call(bf16[16,8,2048]{2,1,0:T(8,128)(2,1)S(1)} %copy-done.1, f32[8,16]{1,0:T(8,128)S(1)} %bitcast.1, bf16[8,128,256]{2,1,0:T(8,128)(2,1)S(1)} %copy-done.2, f32[128,4096]{1,0:T(8,128)S(1)} %copy-done), custom_call_target="tpu_custom_call" | custom-call | tf_op jit(solution)/shard_map/pallas_call | solution.py:292
  61.1 0.8 %copy.6 = bf16[8,128,256]{2,1,0:T(8,128)(2,1)} copy(bf16[8,128,256]{2,1,0:T(8,128)(2,1)S(1)} %shard_map.46) | data formatting | bytes 1048576
Async XLA Ops:
  0.0 1.6 %copy-start = (f32[128,4096]{1,0:T(8,128)S(1)}, f32[128,4096]{1,0:T(8,128)}, u32[]{:S(2)}) copy-start(f32[128,4096]{1,0:T(8,128)} %inverses_hbm.1) | copy-start | bytes 6291460
  1.6 1.0 %copy-start.1 = (bf16[16,8,2048]{2,1,0:T(8,128)(2,1)S(1)}, bf16[16,8,2048]{2,1,0:T(8,128)(2,1)}, u32[]{:S(2)}) copy-start(bf16[16,8,2048]{2,1,0:T(8,128)(2,1)} %grid_hbm.1) | copy-start | bytes 1572868
  2.6 1.0 %copy-start.2 = (bf16[8,128,256]{2,1,0:T(8,128)(2,1)S(1)}, bf16[8,128,256]{2,1,0:T(8,128)(2,1)}, u32[]{:S(2)}) copy-start(bf16[8,128,256]{2,1,0:T(8,128)(2,1)} %weights_hbm.1) | copy-start | bytes 1572868
  3.7 0.7 %copy-start.3 = (f32[16,8]{0,1:T(8,128)S(1)}, f32[16,8]{0,1:T(8,128)}, u32[]{:S(2)}) copy-start(f32[16,8]{0,1:T(8,128)} %param.5) | copy-start | bytes 1540

commit v2 on v1

--- a/solution.py
+++ b/solution.py
@@ -27,10 +27,10 @@
 
 
 def kernel(
-    tasks, grid_hbm, omega_ref, weights_hbm, inverses_hbm, out_ref,
-    grid_v, omega_v, send, recv, weights, flat_inverses, paired_inverses,
+    tasks, grid_hbm, omega_hbm, weights_hbm, inverses_hbm, out_ref,
+    grid_v, omega_ref, omega_v, send, recv, weights, flat_inverses, paired_inverses,
     flip, spread, sym_anti, spec_send, spec_recv, merge, upper, lower, upper_out, lower_out, finish,
-    grid_sem, inv_sem, own_sem, send_sem, recv_sem, wsend_sem, wrecv_sem, ysend_sem, yrecv_sem, yown_sem,
+    grid_sem, omega_sem, inv_sem, own_sem, send_sem, recv_sem, wsend_sem, wrecv_sem, wrelay_sem, ysend_sem, yrecv_sem, ready_sem,
 ):
     row = lax.axis_index("row")
     task = lax.axis_index("ta")
@@ -50,15 +50,42 @@
 
     barrier = pltpu.get_barrier_semaphore()
 
-    @pl.loop(1, tasks)
-    def _(offset):
-        pl.semaphore_signal(barrier, 1, device_id={"ta": lax.rem(task + offset, tasks)}, device_id_type=MESH)
+
+    planes = max(tasks // 8, 1)
+    width = tasks // planes
+    levels = planes // 2 + 1
+    plane, place = task // width, task % width
+
+    def distance(z):
+        return z + z // levels * (planes - 2 * z)
+
+    level = distance(plane)
+
+    def peers(lev, act):
+        for side in range(2):
+            z = lev if side == 0 else planes - lev
+
+            @pl.when((side == 0) | ((lev > 0) & (2 * lev < planes)))
+            def _():
+                @pl.loop(0, width)
+                def _(i):
+                    to = z * width + lax.rem(place + i, width)
+
+                    @pl.when(to != task)
+                    def _():
+                        act(to)
+
+    @pl.loop(level, levels)
+    def _(lev):
+        peers(lev, lambda to: pl.semaphore_signal(barrier, 1, device_id={"ta": to}, device_id_type=MESH))
 
     for offset in range(1, ROWS):
         pl.semaphore_signal(barrier, 1, device_id={"row": lax.rem(row + offset, ROWS)}, device_id_type=MESH)
 
     grid_copy = pltpu.make_async_copy(grid_hbm, grid_v, grid_sem)
     grid_copy.start()
+    omega_copy = pltpu.make_async_copy(omega_hbm, omega_ref, omega_sem)
+    omega_copy.start()
 
     def unit_source(unit, u):
         slot = 2 * u + (1 if unit == 2 else 0)
@@ -73,6 +100,30 @@
             inverses_hbm.at[:, pl.ds(i * LANES, LANES)], flat_inverses.at[:, i, :], inv_sem
         ).start()
 
+    known = 2 * level + 1
+    pl.semaphore_wait(barrier, (known - known // (planes + 1)) * width - 1 + ROWS - 1)
+
+    @pl.loop(0, level)
+    def _(lev):
+        peers(lev, lambda to: pl.semaphore_signal(ready_sem.at[level], 1, device_id={"ta": to}, device_id_type=MESH))
+
+
+    for offset in (1, ROWS - 1):
+        for unit in range(3):
+
+            @when(alive(unit, row))
+            def _():
+                for u in range(4):
+                    pltpu.make_async_remote_copy(
+                        src_ref=unit_source(unit, u),
+                        dst_ref=weights.at[unit, row, u],
+                        send_sem=wsend_sem.at[unit],
+                        recv_sem=wrecv_sem.at[offset, unit],
+                        device_id={"row": lax.rem(row + offset, ROWS)},
+                        device_id_type=MESH,
+                    ).start()
+
+    omega_copy.wait()
     for r in range(16):
         omega_v[pl.ds(8 * r, 8), :] = jnp.broadcast_to(omega_ref[:, r : r + 1], (8, LANES))
     grid_copy.wait()
@@ -103,26 +154,7 @@
             send[group * 4 + d, :, :LANES] = packed[d][:16].astype(BF16)
             send[group * 4 + d, :, LANES:] = packed[d][16:].astype(BF16)
 
-    pl.semaphore_wait(barrier, tasks - 1 + ROWS - 1)
-
-    for offset in range(1, ROWS):
-        for unit in range(3):
-
-            @when(alive(unit, row))
-            def _():
-                for u in range(4):
-                    pltpu.make_async_remote_copy(
-                        src_ref=unit_source(unit, u),
-                        dst_ref=weights.at[unit, row, u],
-                        send_sem=wsend_sem.at[unit],
-                        recv_sem=wrecv_sem.at[offset, unit],
-                        device_id={"row": lax.rem(row + offset, ROWS)},
-                        device_id_type=MESH,
-                    ).start()
-
-    @pl.loop(1, tasks)
-    def _(step):
-        to = lax.rem(task + step, tasks)
+    def deliver(to):
         pltpu.make_async_remote_copy(
             src_ref=send.at[to],
             dst_ref=recv.at[task],
@@ -131,6 +163,14 @@
             device_id={"ta": to},
             device_id_type=MESH,
         ).start()
+
+    for lev in range(levels):
+
+        @pl.when(lev > level)
+        def _():
+            pl.semaphore_wait(ready_sem.at[lev], width * (2 if 0 < 2 * lev < planes else 1))
+
+        peers(lev, deliver)
 
     recv[task] = send[task]
 
@@ -156,25 +196,51 @@
 
     pltpu.make_async_copy(flat_inverses, flat_inverses, inv_sem).wait()
 
-    @pl.loop(0, 2 * block)
-    def _(k):
-        b = flat_inverses[k]
-        rolled = pltpu.roll(b, 64, 1)
-        left = iota((1, LANES), 1) < 64
-        paired_inverses[k] = jnp.concatenate(
-            [jnp.where(left, b, 0.0), jnp.where(left, rolled, 0.0), jnp.where(left, 0.0, rolled), jnp.where(left, 0.0, b)], 0
-        ).astype(BF16)
+    def pair_inverses(start):
+        @pl.loop(start // 4, (start + block) // 4)
+        def _(step):
+            for i in range(4):
+                k = step * 4 + i
+                b = flat_inverses[k]
+                rolled = pltpu.roll(b, 64, 1)
+                left = iota((1, LANES), 1) < 64
+                quarters = (
+                    jnp.where(left, b, 0.0), jnp.where(left, rolled, 0.0),
+                    jnp.where(left, 0.0, rolled), jnp.where(left, 0.0, b),
+                )
+                paired_inverses[k] = jnp.concatenate(quarters, 0).astype(BF16)
+
+    def relay(unit, source, to):
+        @when(alive(unit, source))
+        def _():
+            block_ref = weights.at[unit, source]
+            pltpu.make_async_copy(block_ref, block_ref, wrecv_sem.at[1 if unit == 0 else 3, unit]).wait()
+            pltpu.make_async_remote_copy(
+                src_ref=block_ref,
+                dst_ref=block_ref,
+                send_sem=wrelay_sem.at[unit],
+                recv_sem=wrecv_sem.at[2, unit],
+                device_id={"row": to},
+                device_id_type=MESH,
+            ).start()
+
+    right, left_row, across = (lax.rem(row + i, ROWS) for i in (1, 3, 2))
+    pair_inverses(0)
+    relay(0, left_row, right)
+    relay(1, right, left_row)
+    relay(2, right, left_row)
+    pair_inverses(block)
 
     pltpu.make_async_copy(weights.at[:, 0], weights.at[:, 0], own_sem).wait()
-    for offset in range(1, ROWS):
-        source = lax.rem(row + ROWS - offset, ROWS)
+    for offset, source in ((1, left_row), (2, across), (3, right)):
         for unit in range(3):
+            if offset != 2 and (offset == 1) == (unit == 0):
+                continue
 
             @when(alive(unit, source))
             def _():
-                pltpu.make_async_copy(
-                    weights.at[unit, source], weights.at[unit, source], wrecv_sem.at[offset, unit]
-                ).wait()
+                block_ref = weights.at[unit, source]
+                pltpu.make_async_copy(block_ref, block_ref, wrecv_sem.at[offset, unit]).wait()
 
     pltpu.make_async_copy(recv.at[pl.ds(0, tasks - 1)], recv.at[pl.ds(0, tasks - 1)], recv_sem).wait()
 
@@ -247,15 +313,14 @@
             lhs.astype(BF16), paired_inverses[k], (((1,), (1,)), ((), ())), preferred_element_type=F32
         )
 
-    @pl.loop(0, block)
-    def _(k):
-        solved = solve(upper[pl.ds(pl.multiple_of(k * 16, 16), 16), :], block + k)
-        upper_out[pl.ds(k, 16, stride=block), :] = solved
-
-    @pl.loop(0, block)
-    def _(k):
-        solved = solve(lower[pl.ds(pl.multiple_of(k * 8, 8), 8), :], k)
-        lower_out[pl.ds(k, 8, stride=block), :] = solved
+    @pl.loop(0, block // 4)
+    def _(step):
+        for i in range(4):
+            k = step * 4 + i
+            solved = solve(upper[pl.ds(pl.multiple_of(k * 16, 16), 16), :], block + k)
+            upper_out[pl.ds(k, 16, stride=block), :] = solved
+            solved = solve(lower[pl.ds(pl.multiple_of(k * 8, 8), 8), :], k)
+            lower_out[pl.ds(k, 8, stride=block), :] = solved
 
     def ordered(ref, place):
         fields = [ref[pl.ds((place + field) * block, block), :] for field in range(2)]
@@ -271,8 +336,13 @@
 
         @when(alive(unit, row))
         def _():
-            three = weights.at[unit, pl.ds(0, 3)]
-            pltpu.make_async_copy(three, three, wsend_sem.at[unit]).wait()
+            sent = weights.at[unit, pl.ds(0, 2)]
+            pltpu.make_async_copy(sent, sent, wsend_sem.at[unit]).wait()
+
+        @when(alive(unit, left_row if unit == 0 else right))
+        def _():
+            sent = weights.at[unit, 0]
+            pltpu.make_async_copy(sent, sent, wrelay_sem.at[unit]).wait()
 
         for offset in range(1, ROWS):
             to = lax.rem(row + offset, ROWS)
@@ -286,16 +356,17 @@
 def shards(tasks, grid, omega, legendre_weights, radial_inverses):
     block = tasks
     half_lats = 4 * tasks
-    any_space = pl.BlockSpec(memory_space=pl.ANY)
+    in_hbm = pl.BlockSpec(memory_space=pltpu.HBM)
     in_vmem = pl.BlockSpec(memory_space=pltpu.VMEM)
     dma = pltpu.SemaphoreType.DMA
     return pl.pallas_call(
         functools.partial(kernel, tasks),
         out_shape=jax.ShapeDtypeStruct(legendre_weights.shape[:2] + (256,), BF16),
-        in_specs=[any_space, in_vmem, any_space, any_space],
+        in_specs=[in_hbm] * 4,
         out_specs=in_vmem,
         scratch_shapes=[
             pltpu.VMEM((16, 8, 32 * tasks), BF16),
+            pltpu.VMEM((8, 16), F32),
             pltpu.VMEM((128, LANES), F32),
             pltpu.VMEM((tasks, 16, 256), BF16),
             pltpu.VMEM((tasks, 16, 256), BF16),
@@ -313,11 +384,12 @@
             pltpu.VMEM((block * 16, LANES), F32),
             pltpu.VMEM((block * 8, LANES), F32),
             pltpu.VMEM((256, 256), BF16),
-            dma, dma, dma, dma, dma,
-            dma((3,)), dma((ROWS, 3)), dma((3, ROWS)), dma((3, ROWS)), dma,
+            dma, dma, dma, dma, dma, dma,
+            dma((3,)), dma((ROWS, 3)), dma((3,)), dma((3, ROWS)), dma((3, ROWS)),
+            pltpu.SemaphoreType.REGULAR((5,)),
         ],
         compiler_params=pltpu.CompilerParams(
-            collective_id=0, has_side_effects=True, vmem_limit_bytes=48 * 1024 * 1024
+            collective_id=0, has_side_effects=True, vmem_limit_bytes=60 * 1024 * 1024
         ),
     )(grid, omega.T, legendre_weights, radial_inverses)
 

time: 63 us -> 42.4 us (0.67)
  Pallas kernels: 56.7 us -> 39.7 us
  local copies, waits for them, and re-layouts: 5.15 us -> 1.87 us
    pallas_call x1, Pallas kernels: 56.7 us -> 39.7 us  [shards(): pl.pallas_call(functools.partial(kernel, tasks), out_shape=jax.ShapeDtype...]
    unnamed x9 -> x1, local copies, waits for them, and re-layouts: 5.15 us -> 1.87 us
where the time goes in v2:
time: 42.4 us; the launch traced here: 41.6 us
  Pallas kernels  39.7 us (94%)
  local copies, waits for them, and re-layouts  1.87 us (4%)
    pallas_call x1, Pallas kernels, shards(): pl.pallas_call(functools.partial(kernel, tasks), out_shape=jax.ShapeDtype...  39.7 us
    unnamed x1, local copies, waits for them, and re-layouts  1.87 us

profile of v2, /device:TPU:1, one launch (start us, length us, event | category | flops | bytes accessed | tf_op | source)
XLA Modules:
  0.0 41.6 jit_solution(2731954898659474043)
XLA Ops:
  0.0 39.7 %shard_map.46 = bf16[8,128,256]{2,1,0:T(8,128)(2,1)} custom-call(bf16[16,8,2048]{2,1,0:T(8,128)(2,1)} %grid_hbm.1, f32[8,16]{1,0:T(8,128)} %bitcast.1, bf16[8,128,256]{2,1,0:T(8,128)(2,1)} %weights_hbm.1, f32[128,4096]{1,0:T(8,128)} %inverses_hbm.1), custom_call_target="tpu_custom_call" | custom-call | tf_op jit(solution)/shard_map/pallas_call | solution.py:362
  39.7 1.9 %copy.6 = bf16[8,128,256]{2,1,0:T(8,128)(2,1)} copy(bf16[8,128,256]{2,1,0:T(8,128)(2,1)} %shard_map.46) | data formatting | bytes 1048576

commit v3 on v2

v3 whole, which is shorter than its diff:
```python
import functools

import jax
import jax.numpy as jnp
from jax import lax
from jax.experimental import pallas as pl
from jax.experimental.pallas import tpu as pltpu
from jax.sharding import PartitionSpec as P

MESH = pl.DeviceIdType.MESH
F32 = jnp.float32
BF16 = jnp.bfloat16
ROWS = 4
LANES = 128


def dot(a, b):
    return jnp.dot(a, b, preferred_element_type=F32)


def iota(shape, dim):
    return lax.broadcasted_iota(jnp.int32, shape, dim)


def one_hot(target, width):
    return jnp.where(target == iota((target.shape[0], width), 1), 1.0, 0.0).astype(BF16)


def kernel(
    tasks, grid_hbm, omega_hbm, weights_hbm, inverses_hbm, out_ref,
    grid_v, omega_ref, omega_v, send, recv, weights, flat_inverses, paired_inverses,
    flip, spread, sym_anti, spec_send, spec_recv, merge, spectra, solved, finish,
    grid_sem, omega_sem, inv_sem, own_sem, send_sem, recv_sem, wsend_sem, wrecv_sem, wrelay_sem, ysend_sem, yrecv_sem,
):
    row = lax.axis_index("row")
    task = lax.axis_index("ta")
    block = tasks
    half_lats = 4 * tasks
    orders = 8 * tasks
    groups = tasks // 4
    diagonal = (4 * task) // block

    def alive(unit, r):
        if unit == 0:
            return True
        return r >= diagonal if unit == 1 else r <= diagonal

    def when(condition):
        return (lambda f: f()) if condition is True else pl.when(condition)

    barrier = pltpu.get_barrier_semaphore()

    @pl.loop(1, tasks)
    def _(offset):
        pl.semaphore_signal(barrier, 1, device_id={"ta": lax.rem(task + offset, tasks)}, device_id_type=MESH)

    for offset in range(1, ROWS):
        pl.semaphore_signal(barrier, 1, device_id={"row": lax.rem(row + offset, ROWS)}, device_id_type=MESH)

    grid_copy = pltpu.make_async_copy(grid_hbm, grid_v, grid_sem)
    grid_copy.start()
    omega_copy = pltpu.make_async_copy(omega_hbm, omega_ref, omega_sem)
    omega_copy.start()

    def unit_source(unit, u):
        slot = 2 * u + (1 if unit == 2 else 0)
        first = 0 if unit == 1 else block
        return weights_hbm.at[slot, pl.ds(first, block), :]

    for unit in range(3):
        for u in range(4):
            pltpu.make_async_copy(unit_source(unit, u), weights.at[unit, row, u], own_sem).start()
    for i in range(32):
        pltpu.make_async_copy(
            inverses_hbm.at[:, pl.ds(i * LANES, LANES)], flat_inverses.at[:, i, :], inv_sem
        ).start()

    omega_copy.wait()
    for r in range(16):
        omega_v[pl.ds(8 * r, 8), :] = jnp.broadcast_to(omega_ref[:, r : r + 1], (8, LANES))
    grid_copy.wait()

    @pl.loop(0, groups)
    def _(group):
        lanes = pl.ds(pl.multiple_of(group * LANES, LANES), LANES)
        values = grid_v[:, :, lanes].astype(F32).reshape(16 * 8, LANES)
        lane = iota((1, LANES), 1)
        slot = group * 32 + lane // 4
        order = jnp.where(slot % 2 == 0, slot // 2, orders - 1 - slot // 2).astype(F32)
        partner = jnp.where(lane % 2 == 0, pltpu.roll(values, LANES - 1, 1), -pltpu.roll(values, 1, 1))
        forced = values + (omega_v[...] * order) * partner
        t0, t1, t2, t3 = (forced[32 * q : 32 * q + 32] for q in range(4))
        left = lane < 64
        a0 = jnp.where(left, t0, pltpu.roll(t2, 64, 1))
        a2 = jnp.where(left, pltpu.roll(t0, 64, 1), t2)
        a1 = jnp.where(left, t1, pltpu.roll(t3, 64, 1))
        a3 = jnp.where(left, pltpu.roll(t1, 64, 1), t3)
        first = (lane // 32) % 2 == 0
        packed = (
            jnp.where(first, a0, pltpu.roll(a1, 32, 1)),
            jnp.where(first, pltpu.roll(a0, 96, 1), a1),
            jnp.where(first, a2, pltpu.roll(a3, 32, 1)),
            jnp.where(first, pltpu.roll(a2, 96, 1), a3),
        )
        low = (lane // 4) % 2 == 0
        for d in range(4):
            near, far = packed[d][:16], packed[d][16:]
            send[0, group * 4 + d] = jnp.where(low, near, pltpu.roll(far, 4, 1)).astype(BF16)
            send[1, group * 4 + d] = jnp.where(low, pltpu.roll(near, LANES - 4, 1), far).astype(BF16)

    pl.semaphore_wait(barrier, tasks - 1 + ROWS - 1)

    pltpu.make_async_copy(weights.at[:, 0], weights.at[:, 0], own_sem).wait()
    for unit in range(3):

        @when(alive(unit, row))
        def _():
            for offset in (1, ROWS - 1):
                pltpu.make_async_remote_copy(
                    src_ref=weights.at[unit, row],
                    dst_ref=weights.at[unit, row],
                    send_sem=wsend_sem.at[unit],
                    recv_sem=wrecv_sem.at[offset, unit],
                    device_id={"row": lax.rem(row + offset, ROWS)},
                    device_id_type=MESH,
                ).start()

    def deliver(high, to):
        pltpu.make_async_remote_copy(
            src_ref=send.at[high, to],
            dst_ref=recv.at[high, task],
            send_sem=send_sem.at[high],
            recv_sem=recv_sem.at[high],
            device_id={"ta": to},
            device_id_type=MESH,
        ).start()

    planes = max(tasks // 8, 1)
    width = tasks // planes
    plane, place = task // width, task % width
    steps = sorted(range(planes), key=lambda d: -min(d, planes - d))

    for high in range(2):

        @pl.loop(0, width)
        def _(i):
            for d in steps:
                to = lax.rem(plane + d, planes) * width + lax.rem(place + i, width)

                @pl.when(to != task)
                def _():
                    deliver(high, to)

    recv[:, task] = send[:, task]

    n = half_lats
    flip[...] = one_hot(n - 1 - iota((n, 1), 0), n)
    index = iota((256, 1), 0)
    radius = 4 * ((index // 32) % 4) + 2 * ((index // 4) % 2) + index // LANES
    spread[...] = one_hot(((index // 8) % 4) * 64 + (index % 4) * 16 + radius, 256)
    index = iota((512, 1), 0)
    for second in range(2):
        column = ((index // 16) % 4) * 64 + (index // LANES) * 16 + index % 16
        merge[second] = one_hot(jnp.where((index // 64) % 2 == second, column, -1), 256)
    index = iota((256, 1), 0)
    kind = (index // 32) % 4
    finish[...] = one_hot((2 * (index % 32) + kind % 2) * 4 + (index // LANES) * 2 + kind // 2, 256)
    spectra[...] = jnp.zeros_like(spectra)
    for u in range(4):
        out_ref[2 * u + 1, :block, :] = jnp.zeros((block, 256), BF16)

    pltpu.make_async_copy(flat_inverses, flat_inverses, inv_sem).wait()

    def pair_inverses(start):
        @pl.loop(start // 4, (start + block) // 4)
        def _(step):
            lane = iota((1, LANES), 1)
            turned = flat_inverses[pl.ds(step * 4, 4)].reshape(LANES, LANES).T
            for i in range(4):
                even = pltpu.roll(turned[:64], (LANES - 32 * i) % LANES, 1)
                odd = pltpu.roll(turned[64:], (LANES + 32 - 32 * i) % LANES, 1)
                top = jnp.where(lane < 32, even, jnp.where(lane < 64, odd, 0.0))
                paired_inverses[step * 4 + i] = jnp.concatenate([top, pltpu.roll(top, 64, 1)], 0).astype(BF16)

    def relay(unit, source, to):
        @when(alive(unit, source))
        def _():
            block_ref = weights.at[unit, source]
            pltpu.make_async_copy(block_ref, block_ref, wrecv_sem.at[1 if unit == 0 else 3, unit]).wait()
            pltpu.make_async_remote_copy(
                src_ref=block_ref,
                dst_ref=block_ref,
                send_sem=wrelay_sem.at[unit],
                recv_sem=wrecv_sem.at[2, unit],
                device_id={"row": to},
                device_id_type=MESH,
            ).start()

    right, left_row, across = (lax.rem(row + i, ROWS) for i in (1, 3, 2))
    pair_inverses(0)
    relay(0, left_row, right)
    relay(1, right, left_row)
    relay(2, right, left_row)
    pair_inverses(block)

    def weights_here(unit):
        for offset, source in ((1, left_row), (2, across), (3, right)):
            if offset != 2 and (offset == 1) == (unit == 0):
                continue

            @when(alive(unit, source))
            def _():
                block_ref = weights.at[unit, source]
                pltpu.make_async_copy(block_ref, block_ref, wrecv_sem.at[offset, unit]).wait()

    def separate(high):
        rest = recv.at[high, pl.ds(0, tasks - 1)]
        pltpu.make_async_copy(rest, rest, recv_sem.at[high]).wait()
        arrived = recv[high].astype(F32)
        halves = [arrived[:, 8 * h : 8 * h + 8, :].reshape(2 * half_lats, LANES) for h in range(2)]
        northern = jnp.concatenate([half[:half_lats] for half in halves], 1)
        southern = jnp.concatenate([half[half_lats:] for half in halves], 1)
        southern = dot(flip[...], southern.astype(BF16))
        for which, part in enumerate((northern + southern, northern - southern)):
            columns = dot(part.astype(BF16), spread[...]).astype(BF16)
            for pair in range(2):
                sym_anti[high, pair, :, pl.ds(which * LANES, LANES)] = columns[:, pair * LANES : (pair + 1) * LANES]

    even_row = iota((4 * block, 1), 0) % 2 == 0
    left = iota((1, LANES), 1) < 64

    def transform(unit):
        high = 1 if unit == 2 else 0
        for pair in range(2):
            data = sym_anti[high, pair]
            results = []
            for which in range(2):
                both = dot(weights[unit, :, 2 * pair + which].reshape(4 * block, half_lats), data)
                even_order = (which + high) % 2 == 0
                first, second = both[:, :LANES], both[:, LANES:]
                results.append(jnp.where(even_row, first, second) if even_order else jnp.where(even_row, second, first))
            merged = jnp.where(left, results[0], results[1]).astype(BF16)
            spec_send[unit, :, pair] = merged.reshape(4, block, LANES)
        for offset in (2, 1, 3):
            to = lax.rem(row + offset, ROWS)

            @when(alive(unit, to))
            def _():
                pltpu.make_async_remote_copy(
                    src_ref=spec_send.at[unit, to],
                    dst_ref=spec_recv.at[unit, row],
                    send_sem=ysend_sem.at[unit, offset],
                    recv_sem=yrecv_sem.at[unit, offset],
                    device_id={"row": to},
                    device_id_type=MESH,
                ).start()

        spec_recv[unit, row] = spec_send[unit, row]

    weights_here(0)
    weights_here(1)
    separate(0)
    transform(0)
    transform(1)
    weights_here(2)
    separate(1)
    transform(2)

    def arrive(unit):
        @when(alive(unit, row))
        def _():
            for offset in range(1, ROWS):
                source = lax.rem(row + ROWS - offset, ROWS)
                pltpu.make_async_copy(
                    spec_recv.at[unit, source], spec_recv.at[unit, source], yrecv_sem.at[unit, offset]
                ).wait()
            for pair in range(2):
                joined = jnp.concatenate([spec_recv[unit, r, pair] for r in range(ROWS)], 1)
                for second in range(2):
                    spectrum = dot(joined, merge[second])
                    for field in range(2):
                        spot = (2 * pair + second) * 2 + field
                        spectra[unit, pl.ds(spot, block, stride=8), :] = spectrum[:, field * LANES : (field + 1) * LANES]

    def solve(unit):
        arrive(unit)
        start = 0 if unit == 1 else block
        unroll = min(32, block)

        @pl.loop(0, block // unroll)
        def _(step):
            for i in range(unroll):
                k = step * unroll + i
                lhs = spectra[unit, pl.ds(pl.multiple_of(k * 8, 8), 8), :].astype(BF16)
                solved[unit, pl.ds(k, 8, stride=block), :] = dot(lhs, paired_inverses[start + k])

        for u in range(4):
            fields = [solved[unit, pl.ds((2 * u + field) * block, block), :] for field in range(2)]
            result = dot(jnp.concatenate(fields, 1).astype(BF16), finish[...]).astype(BF16)
            out_ref[2 * u + (1 if unit == 2 else 0), pl.ds(start, block), :] = result

    solve(0)
    solve(1)
    solve(2)

    for high in range(2):
        sent = send.at[high, pl.ds(0, tasks - 1)]
        pltpu.make_async_copy(sent, sent, send_sem.at[high]).wait()
    for unit in range(3):

        @when(alive(unit, row))
        def _():
            sent = weights.at[unit, pl.ds(0, 2)]
            pltpu.make_async_copy(sent, sent, wsend_sem.at[unit]).wait()

        @when(alive(unit, left_row if unit == 0 else right))
        def _():
            sent = weights.at[unit, 0]
            pltpu.make_async_copy(sent, sent, wrelay_sem.at[unit]).wait()

        for offset in range(1, ROWS):
            to = lax.rem(row + offset, ROWS)

            @when(alive(unit, to))
            def _():
                sent = spec_send.at[unit, to]
                pltpu.make_async_copy(sent, sent, ysend_sem.at[unit, offset]).wait()


def shards(tasks, grid, omega, legendre_weights, radial_inverses):
    block = tasks
    half_lats = 4 * tasks
    in_hbm = pl.BlockSpec(memory_space=pltpu.HBM)
    in_vmem = pl.BlockSpec(memory_space=pltpu.VMEM)
    dma = pltpu.SemaphoreType.DMA
    return pl.pallas_call(
        functools.partial(kernel, tasks),
        out_shape=jax.ShapeDtypeStruct(legendre_weights.shape[:2] + (256,), BF16),
        in_specs=[in_hbm] * 4,
        out_specs=in_vmem,
        scratch_shapes=[
            pltpu.VMEM((16, 8, 32 * tasks), BF16),
            pltpu.VMEM((8, 16), F32),
            pltpu.VMEM((128, LANES), F32),
            pltpu.VMEM((2, tasks, 16, LANES), BF16),
            pltpu.VMEM((2, tasks, 16, LANES), BF16),
            pltpu.VMEM((3, ROWS, 4, block, half_lats), BF16),
            pltpu.VMEM((2 * block, 32, LANES), F32),
            pltpu.VMEM((2 * block, LANES, LANES), BF16),
            pltpu.VMEM((half_lats, half_lats), BF16),
            pltpu.VMEM((256, 256), BF16),
            pltpu.VMEM((2, 2, half_lats, 256), BF16),
            pltpu.VMEM((3, ROWS, 2, block, LANES), BF16),
            pltpu.VMEM((3, ROWS, 2, block, LANES), BF16),
            pltpu.VMEM((2, 512, 256), BF16),
            pltpu.VMEM((3, block * 8, LANES), F32),
            pltpu.VMEM((3, block * 8, LANES), F32),
            pltpu.VMEM((256, 256), BF16),
            dma, dma, dma, dma, dma((2,)), dma((2,)),
            dma((3,)), dma((ROWS, 3)), dma((3,)), dma((3, ROWS)), dma((3, ROWS)),
        ],
        compiler_params=pltpu.CompilerParams(
            collective_id=0, has_side_effects=True, vmem_limit_bytes=60 * 1024 * 1024
        ),
    )(grid, omega.T, legendre_weights, radial_inverses)


def solution(mesh):
    in_specs = (P("row", "ta", None), P("row", "ta"), P("ta", "row", None), P("row", None))
    out_specs = P("ta", "row", None)
    return jax.shard_map(
        functools.partial(shards, mesh.shape["ta"]), mesh=mesh, in_specs=in_specs, out_specs=out_specs, check_vma=False
    )
```

time: 42.4 us -> 39 us (0.920); the launches traced: 41.6 us -> 38.9 us
  Pallas kernels: 39.7 us -> 37 us
    pallas_call x1, Pallas kernels: 39.7 us -> 37 us  [shards(): pl.pallas_call(functools.partial(kernel, tasks), out_shape=jax.ShapeDtype...]
where the time goes in v3:
time: 39 us; the launch traced here: 38.9 us
  Pallas kernels  37 us (95%)
  local copies, waits for them, and re-layouts  1.87 us (5%)
    pallas_call x1, Pallas kernels, shards(): pl.pallas_call(functools.partial(kernel, tasks), out_shape=jax.ShapeDtype...  37 us
    unnamed x1, local copies, waits for them, and re-layouts  1.87 us

profile of v3, /device:TPU:1, one launch (start us, length us, event | category | flops | bytes accessed | tf_op | source)
XLA Modules:
  0.0 38.9 jit_solution(11782659753114738565)
XLA Ops:
  0.0 37.0 %shard_map.46 = bf16[8,128,256]{2,1,0:T(8,128)(2,1)} custom-call(bf16[16,8,2048]{2,1,0:T(8,128)(2,1)} %grid_hbm.1, f32[8,16]{1,0:T(8,128)} %bitcast.1, bf16[8,128,256]{2,1,0:T(8,128)(2,1)} %weights_hbm.1, f32[128,4096]{1,0:T(8,128)} %inverses_hbm.1), custom_call_target="tpu_custom_call" | custom-call | tf_op jit(solution)/shard_map/pallas_call | solution.py:336
  37.0 1.9 %copy.6 = bf16[8,128,256]{2,1,0:T(8,128)(2,1)} copy(bf16[8,128,256]{2,1,0:T(8,128)(2,1)} %shard_map.46) | data formatting | bytes 1048576

commit v4 on v3

--- a/solution.py
+++ b/solution.py
@@ -28,7 +28,7 @@
 
 def kernel(
     tasks, grid_hbm, omega_hbm, weights_hbm, inverses_hbm, out_ref,
-    grid_v, omega_ref, omega_v, send, recv, weights, flat_inverses, paired_inverses,
+    turn, grid_v, omega_ref, omega_v, send, recv, weights, flat_inverses, paired_inverses,
     flip, spread, sym_anti, spec_send, spec_recv, merge, spectra, solved, finish,
     grid_sem, omega_sem, inv_sem, own_sem, send_sem, recv_sem, wsend_sem, wrecv_sem, wrelay_sem, ysend_sem, yrecv_sem,
 ):
@@ -48,19 +48,20 @@
     def when(condition):
         return (lambda f: f()) if condition is True else pl.when(condition)
 
-    barrier = pltpu.get_barrier_semaphore()
-
-    @pl.loop(1, tasks)
-    def _(offset):
-        pl.semaphore_signal(barrier, 1, device_id={"ta": lax.rem(task + offset, tasks)}, device_id_type=MESH)
-
-    for offset in range(1, ROWS):
-        pl.semaphore_signal(barrier, 1, device_id={"row": lax.rem(row + offset, ROWS)}, device_id_type=MESH)
-
     grid_copy = pltpu.make_async_copy(grid_hbm, grid_v, grid_sem)
     grid_copy.start()
     omega_copy = pltpu.make_async_copy(omega_hbm, omega_ref, omega_sem)
     omega_copy.start()
+
+    barrier = pltpu.get_barrier_semaphore()
+
+    @pl.loop(1, tasks)
+    def _(offset):
+        pl.semaphore_signal(barrier, 1, device_id={"ta": lax.rem(task + offset, tasks)}, device_id_type=MESH)
+
+    for offset in range(1, ROWS):
+        pl.semaphore_signal(barrier, 1, device_id={"row": lax.rem(row + offset, ROWS)}, device_id_type=MESH)
+
 
     def unit_source(unit, u):
         slot = 2 * u + (1 if unit == 2 else 0)
@@ -75,83 +76,46 @@
             inverses_hbm.at[:, pl.ds(i * LANES, LANES)], flat_inverses.at[:, i, :], inv_sem
         ).start()
 
+    source = iota((LANES, LANES), 0)
+    target = iota((LANES, LANES), 1)
+    sign = jnp.where(target % 2 == 0, 1.0, -1.0)
+    turn[...] = jnp.where(source == target + 1 - 2 * (target % 2), sign, 0.0).astype(BF16)
     omega_copy.wait()
     for r in range(16):
         omega_v[pl.ds(8 * r, 8), :] = jnp.broadcast_to(omega_ref[:, r : r + 1], (8, LANES))
     grid_copy.wait()
 
-    @pl.loop(0, groups)
-    def _(group):
-        lanes = pl.ds(pl.multiple_of(group * LANES, LANES), LANES)
-        values = grid_v[:, :, lanes].astype(F32).reshape(16 * 8, LANES)
-        lane = iota((1, LANES), 1)
-        slot = group * 32 + lane // 4
-        order = jnp.where(slot % 2 == 0, slot // 2, orders - 1 - slot // 2).astype(F32)
-        partner = jnp.where(lane % 2 == 0, pltpu.roll(values, LANES - 1, 1), -pltpu.roll(values, 1, 1))
-        forced = values + (omega_v[...] * order) * partner
-        t0, t1, t2, t3 = (forced[32 * q : 32 * q + 32] for q in range(4))
-        left = lane < 64
-        a0 = jnp.where(left, t0, pltpu.roll(t2, 64, 1))
-        a2 = jnp.where(left, pltpu.roll(t0, 64, 1), t2)
-        a1 = jnp.where(left, t1, pltpu.roll(t3, 64, 1))
-        a3 = jnp.where(left, pltpu.roll(t1, 64, 1), t3)
-        first = (lane // 32) % 2 == 0
-        packed = (
-            jnp.where(first, a0, pltpu.roll(a1, 32, 1)),
-            jnp.where(first, pltpu.roll(a0, 96, 1), a1),
-            jnp.where(first, a2, pltpu.roll(a3, 32, 1)),
-            jnp.where(first, pltpu.roll(a2, 96, 1), a3),
-        )
-        low = (lane // 4) % 2 == 0
-        for d in range(4):
-            near, far = packed[d][:16], packed[d][16:]
-            send[0, group * 4 + d] = jnp.where(low, near, pltpu.roll(far, 4, 1)).astype(BF16)
-            send[1, group * 4 + d] = jnp.where(low, pltpu.roll(near, LANES - 4, 1), far).astype(BF16)
-
-    pl.semaphore_wait(barrier, tasks - 1 + ROWS - 1)
-
-    pltpu.make_async_copy(weights.at[:, 0], weights.at[:, 0], own_sem).wait()
-    for unit in range(3):
-
-        @when(alive(unit, row))
-        def _():
-            for offset in (1, ROWS - 1):
-                pltpu.make_async_remote_copy(
-                    src_ref=weights.at[unit, row],
-                    dst_ref=weights.at[unit, row],
-                    send_sem=wsend_sem.at[unit],
-                    recv_sem=wrecv_sem.at[offset, unit],
-                    device_id={"row": lax.rem(row + offset, ROWS)},
-                    device_id_type=MESH,
-                ).start()
-
-    def deliver(high, to):
-        pltpu.make_async_remote_copy(
-            src_ref=send.at[high, to],
-            dst_ref=recv.at[high, task],
-            send_sem=send_sem.at[high],
-            recv_sem=recv_sem.at[high],
-            device_id={"ta": to},
-            device_id_type=MESH,
-        ).start()
-
-    planes = max(tasks // 8, 1)
-    width = tasks // planes
-    plane, place = task // width, task % width
-    steps = sorted(range(planes), key=lambda d: -min(d, planes - d))
-
-    for high in range(2):
-
-        @pl.loop(0, width)
-        def _(i):
-            for d in steps:
-                to = lax.rem(plane + d, planes) * width + lax.rem(place + i, width)
-
-                @pl.when(to != task)
-                def _():
-                    deliver(high, to)
-
-    recv[:, task] = send[:, task]
+    lane = iota((1, LANES), 1)
+    left_half = lane < 64
+    first = (lane // 32) % 2 == 0
+    low = (lane // 4) % 2 == 0
+    unroll = min(4, groups)
+
+    @pl.loop(0, groups // unroll)
+    def _(step):
+        for i in range(unroll):
+            group = step * unroll + i
+            lanes = pl.ds(pl.multiple_of(group * LANES, LANES), LANES)
+            values = grid_v[:, :, lanes].astype(F32).reshape(16 * 8, LANES)
+            slot = group * 32 + lane // 4
+            order = jnp.where(slot % 2 == 0, slot // 2, orders - 1 - slot // 2).astype(F32)
+            partner = dot(values.astype(BF16), turn[...])
+            forced = values + (omega_v[...] * order) * partner
+            t0, t1, t2, t3 = (forced[32 * q : 32 * q + 32].astype(BF16) for q in range(4))
+            a0 = jnp.where(left_half, t0, pltpu.roll(t2, 64, 1))
+            a2 = jnp.where(left_half, pltpu.roll(t0, 64, 1), t2)
+            a1 = jnp.where(left_half, t1, pltpu.roll(t3, 64, 1))
+            a3 = jnp.where(left_half, pltpu.roll(t1, 64, 1), t3)
+            packed = (
+                jnp.where(first, a0, pltpu.roll(a1, 32, 1)),
+                jnp.where(first, pltpu.roll(a0, 96, 1), a1),
+                jnp.where(first, a2, pltpu.roll(a3, 32, 1)),
+                jnp.where(first, pltpu.roll(a2, 96, 1), a3),
+            )
+            for d in range(4):
+                near, far = packed[d][:16], packed[d][16:]
+                send[0, group * 4 + d] = jnp.where(low, near, pltpu.roll(far, 4, 1)).astype(BF16)
+                send[1, group * 4 + d] = jnp.where(low, pltpu.roll(near, LANES - 4, 1), far).astype(BF16)
 
     n = half_lats
     flip[...] = one_hot(n - 1 - iota((n, 1), 0), n)
@@ -169,18 +133,70 @@
     for u in range(4):
         out_ref[2 * u + 1, :block, :] = jnp.zeros((block, 256), BF16)
 
+    pl.semaphore_wait(barrier, tasks - 1 + ROWS - 1)
+
+    pltpu.make_async_copy(weights.at[:, 0], weights.at[:, 0], own_sem).wait()
+
+    def offer(unit):
+        @when(alive(unit, row))
+        def _():
+            for offset in (1, ROWS - 1):
+                pltpu.make_async_remote_copy(
+                    src_ref=weights.at[unit, row],
+                    dst_ref=weights.at[unit, row],
+                    send_sem=wsend_sem.at[unit],
+                    recv_sem=wrecv_sem.at[offset, unit],
+                    device_id={"row": lax.rem(row + offset, ROWS)},
+                    device_id_type=MESH,
+                ).start()
+
+    offer(0)
+    offer(1)
+
+    def deliver(high, to):
+        pltpu.make_async_remote_copy(
+            src_ref=send.at[high, to],
+            dst_ref=recv.at[high, task],
+            send_sem=send_sem.at[high],
+            recv_sem=recv_sem.at[high],
+            device_id={"ta": to},
+            device_id_type=MESH,
+        ).start()
+
+    planes = max(tasks // 8, 1)
+    width = tasks // planes
+    plane, place = task // width, task % width
+    steps = sorted(range(planes), key=lambda d: -min(d, planes - d))
+
+    for high in range(2):
+
+        @pl.loop(0, width)
+        def _(i):
+            for d in steps:
+                if d > 0:
+                    deliver(high, lax.rem(plane + d, planes) * width + lax.rem(place + i, width))
+
+        @pl.loop(1, width)
+        def _(i):
+            deliver(high, plane * width + lax.rem(place + i, width))
+
+        if high == 0:
+            offer(2)
+
+    recv[:, task] = send[:, task]
+
     pltpu.make_async_copy(flat_inverses, flat_inverses, inv_sem).wait()
 
     def pair_inverses(start):
         @pl.loop(start // 4, (start + block) // 4)
         def _(step):
             lane = iota((1, LANES), 1)
-            turned = flat_inverses[pl.ds(step * 4, 4)].reshape(LANES, LANES).T
+            turned = flat_inverses[pl.ds(step * 4, 4)].reshape(LANES, LANES).T.astype(BF16)
             for i in range(4):
                 even = pltpu.roll(turned[:64], (LANES - 32 * i) % LANES, 1)
                 odd = pltpu.roll(turned[64:], (LANES + 32 - 32 * i) % LANES, 1)
-                top = jnp.where(lane < 32, even, jnp.where(lane < 64, odd, 0.0))
-                paired_inverses[step * 4 + i] = jnp.concatenate([top, pltpu.roll(top, 64, 1)], 0).astype(BF16)
+                top = jnp.where(lane < 32, even, jnp.where(lane < 64, odd, jnp.zeros_like(odd)))
+                paired_inverses[step * 4 + i] = jnp.concatenate([top, pltpu.roll(top, 64, 1)], 0)
 
     def relay(unit, source, to):
         @when(alive(unit, source))
@@ -200,8 +216,8 @@
     pair_inverses(0)
     relay(0, left_row, right)
     relay(1, right, left_row)
+    pair_inverses(block)
     relay(2, right, left_row)
-    pair_inverses(block)
 
     def weights_here(unit):
         for offset, source in ((1, left_row), (2, across), (3, right)):
@@ -227,8 +243,6 @@
                 sym_anti[high, pair, :, pl.ds(which * LANES, LANES)] = columns[:, pair * LANES : (pair + 1) * LANES]
 
     even_row = iota((4 * block, 1), 0) % 2 == 0
-    left = iota((1, LANES), 1) < 64
-
     def transform(unit):
         high = 1 if unit == 2 else 0
         for pair in range(2):
@@ -239,7 +253,7 @@
                 even_order = (which + high) % 2 == 0
                 first, second = both[:, :LANES], both[:, LANES:]
                 results.append(jnp.where(even_row, first, second) if even_order else jnp.where(even_row, second, first))
-            merged = jnp.where(left, results[0], results[1]).astype(BF16)
+            merged = jnp.where(left_half, results[0], results[1]).astype(BF16)
             spec_send[unit, :, pair] = merged.reshape(4, block, LANES)
         for offset in (2, 1, 3):
             to = lax.rem(row + offset, ROWS)
@@ -339,6 +353,7 @@
         in_specs=[in_hbm] * 4,
         out_specs=in_vmem,
         scratch_shapes=[
+            pltpu.VMEM((LANES, LANES), BF16),
             pltpu.VMEM((16, 8, 32 * tasks), BF16),
             pltpu.VMEM((8, 16), F32),
             pltpu.VMEM((128, LANES), F32),

time: 39 us -> 36.4 us (0.933); the launches traced: 38.9 us -> 35.7 us
  Pallas kernels: 37 us -> 33.8 us
    pallas_call x1, Pallas kernels: 37 us -> 33.8 us  [shards(): pl.pallas_call(functools.partial(kernel, tasks), out_shape=jax.ShapeDtype...]
where the time goes in v4:
time: 36.4 us; the launch traced here: 35.7 us
  Pallas kernels  33.8 us (93%)
  local copies, waits for them, and re-layouts  1.87 us (5%)
    pallas_call x1, Pallas kernels, shards(): pl.pallas_call(functools.partial(kernel, tasks), out_shape=jax.ShapeDtype...  33.8 us
    unnamed x1, local copies, waits for them, and re-layouts  1.87 us

profile of v4, /device:TPU:1, one launch (start us, length us, event | category | flops | bytes accessed | tf_op | source)
XLA Modules:
  0.0 35.7 jit_solution(17986780058141723498)
XLA Ops:
  0.0 33.8 %shard_map.46 = bf16[8,128,256]{2,1,0:T(8,128)(2,1)} custom-call(bf16[16,8,2048]{2,1,0:T(8,128)(2,1)} %grid_hbm.1, f32[8,16]{1,0:T(8,128)} %bitcast.1, bf16[8,128,256]{2,1,0:T(8,128)(2,1)} %weights_hbm.1, f32[128,4096]{1,0:T(8,128)} %inverses_hbm.1), custom_call_target="tpu_custom_call" | custom-call | tf_op jit(solution)/shard_map/pallas_call | solution.py:350
  33.8 1.9 %copy.6 = bf16[8,128,256]{2,1,0:T(8,128)(2,1)} copy(bf16[8,128,256]{2,1,0:T(8,128)(2,1)} %shard_map.46) | data formatting | bytes 1048576

commit v5 on v4

--- a/solution.py
+++ b/solution.py
@@ -192,11 +192,13 @@
         def _(step):
             lane = iota((1, LANES), 1)
             turned = flat_inverses[pl.ds(step * 4, 4)].reshape(LANES, LANES).T.astype(BF16)
+            even = [turned[:64] if r == 0 else pltpu.roll(turned[:64], 32 * r, 1) for r in range(4)]
+            odd = [turned[64:] if r == 0 else pltpu.roll(turned[64:], 32 * r, 1) for r in range(4)]
+            zero = jnp.zeros_like(turned[:64])
             for i in range(4):
-                even = pltpu.roll(turned[:64], (LANES - 32 * i) % LANES, 1)
-                odd = pltpu.roll(turned[64:], (LANES + 32 - 32 * i) % LANES, 1)
-                top = jnp.where(lane < 32, even, jnp.where(lane < 64, odd, jnp.zeros_like(odd)))
-                paired_inverses[step * 4 + i] = jnp.concatenate([top, pltpu.roll(top, 64, 1)], 0)
+                top = jnp.where(lane < 32, even[-i % 4], jnp.where(lane < 64, odd[(1 - i) % 4], zero))
+                bottom = jnp.where(lane < 64, zero, jnp.where(lane < 96, even[(2 - i) % 4], odd[(3 - i) % 4]))
+                paired_inverses[step * 4 + i] = jnp.concatenate([top, bottom], 0)
 
     def relay(unit, source, to):
         @when(alive(unit, source))
@@ -299,7 +301,7 @@
     def solve(unit):
         arrive(unit)
         start = 0 if unit == 1 else block
-        unroll = min(32, block)
+        unroll = min(64, block)
 
         @pl.loop(0, block // unroll)
         def _(step):

time: 36.4 us -> 34.8 us (0.956); the launches traced: 35.7 us -> 34.7 us
  Pallas kernels: 33.8 us -> 32.8 us
    pallas_call x1, Pallas kernels: 33.8 us -> 32.8 us  [shards(): pl.pallas_call(functools.partial(kernel, tasks), out_shape=jax.ShapeDtype...]
where the time goes in v5:
time: 34.8 us; the launch traced here: 34.7 us
  Pallas kernels  32.8 us (94%)
  local copies, waits for them, and re-layouts  1.87 us (5%)
    pallas_call x1, Pallas kernels, shards(): pl.pallas_call(functools.partial(kernel, tasks), out_shape=jax.ShapeDtype...  32.8 us
    unnamed x1, local copies, waits for them, and re-layouts  1.87 us

profile of v5, /device:TPU:1, one launch (start us, length us, event | category | flops | bytes accessed | tf_op | source)
XLA Modules:
  0.0 34.7 jit_solution(183343670300226811)
XLA Ops:
  0.0 32.8 %shard_map.46 = bf16[8,128,256]{2,1,0:T(8,128)(2,1)} custom-call(bf16[16,8,2048]{2,1,0:T(8,128)(2,1)} %grid_hbm.1, f32[8,16]{1,0:T(8,128)} %bitcast.1, bf16[8,128,256]{2,1,0:T(8,128)(2,1)} %weights_hbm.1, f32[128,4096]{1,0:T(8,128)} %inverses_hbm.1), custom_call_target="tpu_custom_call" | custom-call | tf_op jit(solution)/shard_map/pallas_call | solution.py:352
  32.8 1.9 %copy.6 = bf16[8,128,256]{2,1,0:T(8,128)(2,1)} copy(bf16[8,128,256]{2,1,0:T(8,128)(2,1)} %shard_map.46) | data formatting | bytes 1048576

commit v6 on v5

--- a/solution.py
+++ b/solution.py
@@ -370,8 +370,8 @@
             pltpu.VMEM((3, ROWS, 2, block, LANES), BF16),
             pltpu.VMEM((3, ROWS, 2, block, LANES), BF16),
             pltpu.VMEM((2, 512, 256), BF16),
-            pltpu.VMEM((3, block * 8, LANES), F32),
-            pltpu.VMEM((3, block * 8, LANES), F32),
+            pltpu.VMEM((3, block * 8 + 8, LANES), F32),
+            pltpu.VMEM((3, block * 9, LANES), F32),
             pltpu.VMEM((256, 256), BF16),
             dma, dma, dma, dma, dma((2,)), dma((2,)),
             dma((3,)), dma((ROWS, 3)), dma((3,)), dma((3, ROWS)), dma((3, ROWS)),

time: 34.8 us -> 34.8 us (level)
  no operation moved by 1% of the time
where the time goes in v6:
time: 34.8 us; the launch traced here: 34.7 us
  Pallas kernels  32.8 us (94%)
  local copies, waits for them, and re-layouts  1.87 us (5%)
    pallas_call x1, Pallas kernels, shards(): pl.pallas_call(functools.partial(kernel, tasks), out_shape=jax.ShapeDtype...  32.8 us
    unnamed x1, local copies, waits for them, and re-layouts  1.87 us

profile of v6, /device:TPU:1, one launch (start us, length us, event | category | flops | bytes accessed | tf_op | source)
XLA Modules:
  0.0 34.7 jit_solution(1365579553190282693)
XLA Ops:
  0.0 32.8 %shard_map.46 = bf16[8,128,256]{2,1,0:T(8,128)(2,1)} custom-call(bf16[16,8,2048]{2,1,0:T(8,128)(2,1)} %grid_hbm.1, f32[8,16]{1,0:T(8,128)} %bitcast.1, bf16[8,128,256]{2,1,0:T(8,128)(2,1)} %weights_hbm.1, f32[128,4096]{1,0:T(8,128)} %inverses_hbm.1), custom_call_target="tpu_custom_call" | custom-call | tf_op jit(solution)/shard_map/pallas_call | solution.py:352
  32.8 1.9 %copy.6 = bf16[8,128,256]{2,1,0:T(8,128)(2,1)} copy(bf16[8,128,256]{2,1,0:T(8,128)(2,1)} %shard_map.46) | data formatting | bytes 1048576

commit v7 on v6

--- a/solution.py
+++ b/solution.py
@@ -273,13 +273,13 @@
 
         spec_recv[unit, row] = spec_send[unit, row]
 
+    separate(0)
     weights_here(0)
+    transform(0)
     weights_here(1)
-    separate(0)
-    transform(0)
     transform(1)
+    separate(1)
     weights_here(2)
-    separate(1)
     transform(2)
 
     def arrive(unit):

time: 34.8 us -> 34.7 us (level); the launches traced: 34.7 us -> 34.2 us
  Pallas kernels: 32.8 us -> 32.3 us
    pallas_call x1, Pallas kernels: 32.8 us -> 32.3 us  [shards(): pl.pallas_call(functools.partial(kernel, tasks), out_shape=jax.ShapeDtype...]
where the time goes in v7:
time: 34.7 us; the launch traced here: 34.2 us
  Pallas kernels  32.3 us (93%)
  local copies, waits for them, and re-layouts  1.87 us (5%)
    pallas_call x1, Pallas kernels, shards(): pl.pallas_call(functools.partial(kernel, tasks), out_shape=jax.ShapeDtype...  32.3 us
    unnamed x1, local copies, waits for them, and re-layouts  1.87 us

profile of v7, /device:TPU:1, one launch (start us, length us, event | category | flops | bytes accessed | tf_op | source)
XLA Modules:
  0.0 34.2 jit_solution(1265195996050109667)
XLA Ops:
  0.0 32.3 %shard_map.46 = bf16[8,128,256]{2,1,0:T(8,128)(2,1)} custom-call(bf16[16,8,2048]{2,1,0:T(8,128)(2,1)} %grid_hbm.1, f32[8,16]{1,0:T(8,128)} %bitcast.1, bf16[8,128,256]{2,1,0:T(8,128)(2,1)} %weights_hbm.1, f32[128,4096]{1,0:T(8,128)} %inverses_hbm.1), custom_call_target="tpu_custom_call" | custom-call | tf_op jit(solution)/shard_map/pallas_call | solution.py:352
  32.3 1.9 %copy.6 = bf16[8,128,256]{2,1,0:T(8,128)(2,1)} copy(bf16[8,128,256]{2,1,0:T(8,128)(2,1)} %shard_map.46) | data formatting | bytes 1048576
